TPU v7x, 32 devices: a whole 2x2x4 slice. The times are simulated.
32 devices in a mesh: section: 4 (over x, core), seq: 8 (over z, y).
Axes of the slice: x: 2, y: 2, z: 4, core: 2. Of those that a mesh axis runs over, the one named last changes fastest.
Arguments:
- activations: bfloat16 [4, 2048, 1536], P('section', 'seq'), may hold values from -6 to 6
- qkv_weight: bfloat16 [4, 1536, 4608], P('section'), may hold values from -5 to 5
- out_weight: bfloat16 [4, 1536, 1536], P('section'), may hold values from -0.15625 to 0.15625
- modulation: float32 [4, 3, 1536], P('section'), may hold values from -4 to 4
- key_blocks: int32 [16, 4], replicated, may hold values from 0 to 15, as said below
- block_counts: int32 [16], replicated, may hold values from 3 to 4, as said below
Outputs:
- advanced: bfloat16 [4, 2048, 1536], P('section', 'seq')
Inputs may be any that keep to these rules, and one draw needn't show every extreme that they name: Block b belongs to group b // 2. Row b of key_blocks names first its own block, then the other blocks of its group, then 2 blocks of different groups g with 1 <= |g - b // 2| <= 2. All rows of one group name at most one block of any other group. `block_counts`: some query block uses all 4 entries.
All inputs are finite; a program needn't handle non-finite values.
Results may differ from a plain program's by a relative error of at most 0.008.
Values may be sent and summed in bfloat16 or wider, within the bound.
No kernel may reach another device: no remote copies, remote signals or barrier semaphores. Data moves between devices by JAX's collectives and lax.ppermute only.
A program may use at most 128 MiB of HBM per device.

v0:
```python
import functools

import jax
import jax.numpy as jnp
from jax import lax
from jax.experimental import pallas as pl
from jax.experimental.pallas import tpu as pltpu
from jax.sharding import PartitionSpec as P

HEADS = 12
HD = 128
BLK = 128
EPSILON = 1e-06
INNER = HEADS * HD
PAIR = 2 * HD
TO_EXP2 = HD ** (-0.5) * 1.4426950408889634
MASKED = -1e30
FIRST_EARLY, FIRST_LATE = (1,), (0, 2, 3)
SECOND_EARLY, SECOND_LATE = (0, 2, 1), (3,)
SWAPPED = (1,)
PIECES = 2
LIMIT = 16 * 2**20
FIRST_LIMIT = 30 * 2**20

IN_VMEM = pl.BlockSpec(memory_space=pltpu.VMEM)
IN_SMEM = pl.BlockSpec(memory_space=pltpu.SMEM)
IN_HBM = pl.BlockSpec(memory_space=pltpu.HBM)


def beyond(me, count):
    one = me + 1 - 2 * (me % 2)
    other_one = me - 1 + 2 * (me % 2)
    two = me + 2 - 4 * ((me // 2) % 2)
    other_two = me - 2 + 4 * ((me // 2) % 2)
    return [one, other_one, two, other_two]


def partner_table(count):
    table = []
    for me in range(count):
        table.append([p if 0 <= p < count else me for p in beyond(me, count)])
    return table


def pairs_of(exchange, count):
    table = partner_table(count)
    return [(me, table[me][exchange]) for me in range(count)]


def asked_block(key_ref, target, me, blocks_here):
    width = key_ref.shape[0]
    found = jnp.int32(0)
    for row in range(blocks_here):
        for entry in range(width):
            named = key_ref[entry, target * blocks_here + row]
            mine = (named >= me * blocks_here) & (named < (me + 1) * blocks_here)
            found = jnp.where(mine, named - me * blocks_here, found)
    return found


def partners_here(me, count):
    out = []
    for p in beyond(me, count):
        out.append(jnp.where((p >= 0) & (p < count), p, me))
    return out


def pick_kernel(count, exchanges, parts, key_ref, *refs):
    send_asked(count, exchanges, key_ref, refs[:parts], refs[parts:])


def pick_blocks(parts, key_blocks, count, exchanges, params=None):
    width = parts[0].shape[1]
    return pl.pallas_call(
        functools.partial(pick_kernel, count, exchanges, len(parts)),
        out_shape=[jax.ShapeDtypeStruct((BLK, width), parts[0].dtype)] * len(exchanges),
        in_specs=[IN_SMEM] + [IN_VMEM] * len(parts),
        out_specs=[IN_VMEM] * len(exchanges),
        compiler_params=params,
        name="pick_blocks",
    )(key_blocks, *parts)


def send_asked(count, exchanges, key_ref, parts, sends):
    me = lax.axis_index("seq")
    rows = parts[0].shape[0]
    blocks_here = len(parts) * rows // BLK
    for exchange, send in zip(exchanges, sends):
        block = asked_block(key_ref, partners_here(me, count)[exchange], me, blocks_here)
        if len(parts) == 1:
            send[...] = parts[0][pl.ds(pl.multiple_of(block * BLK, BLK), BLK), :]
        else:
            each = BLK // rows
            for n in range(blocks_here):

                @pl.when(block == n)
                def _():
                    for m in range(each):
                        send[m * rows : (m + 1) * rows, :] = parts[n * each + m][...]


def norm_rows(x_ref, mod_ref, out_ref, out_row):
    rows, width = x_ref.shape
    shift = mod_ref[0]
    scale = 1.0 + mod_ref[1]
    step = 16
    for r in range(0, rows, step):
        values = x_ref[r : r + step, :].astype(jnp.float32)
        center = jnp.sum(values, axis=-1, keepdims=True) * (1.0 / width)
        values = values - center
        spread = jnp.sum(values * values, axis=-1, keepdims=True) * (1.0 / width)
        normed = values * lax.rsqrt(spread + EPSILON)
        out_ref[out_row + r : out_row + r + step, :] = (normed * scale + shift).astype(jnp.bfloat16)


def project(source, weight_ref, column, width):
    return jnp.dot(
        source, weight_ref[:, column : column + width], preferred_element_type=jnp.float32
    ).astype(jnp.bfloat16)


def scores_of(q, k):
    return lax.dot_general(q, k, (((1,), (1,)), ((), ())), preferred_element_type=jnp.float32)


def with_ones(v):
    return jnp.concatenate([v, jnp.ones(v.shape, v.dtype)], axis=1)


def own_columns():
    wide = 4 * HD
    for at in range(0, INNER, wide):
        yield at, wide


def own_heads(normed, w_ref, q_ref, kv, peak_ref, total_ref, acc_ref, row, before):
    rows = slice(row, q_ref.shape[0])
    for n, (at, wide) in enumerate(own_columns()):
        cols = slice(at, at + wide)
        before(3 * n)
        q_ref[rows, cols] = project(normed[...], w_ref, at, wide)
        before(3 * n + 1)
        kv[rows, cols] = project(normed[...], w_ref, INNER + at, wide)
        before(3 * n + 2)
        kv[rows, INNER + at : INNER + at + wide] = project(normed[...], w_ref, 2 * INNER + at, wide)
        for h in range(at, at + wide, HD):
            here = slice(h, h + HD)
            s = scores_of(q_ref[:, here], kv[:, here])
            peak = jnp.max(s, axis=-1, keepdims=True)
            p = jnp.exp2((s - peak) * TO_EXP2).astype(jnp.bfloat16)
            both = jnp.dot(p, with_ones(kv[:, INNER + h : INNER + h + HD]), preferred_element_type=jnp.float32)
            peak_ref[:, here] = jnp.broadcast_to(peak, (s.shape[0], HD))
            total_ref[:, here] = both[:, HD:]
            acc_ref[:, here] = both[:, :HD]


def first_kernel(
    x_ref, mod_ref, w_hbm, q_ref, peak_ref, total_ref, acc_ref, w_ref, normed, kv, sems
):
    wide = 4 * HD
    copies = []
    for at in range(0, INNER, wide):
        for c in (at, INNER + at, 2 * INNER + at):
            n = len(copies)
            cols = slice(c, c + wide)
            copies.append(pltpu.make_async_copy(w_hbm.at[:, cols], w_ref.at[:, cols], sems.at[n]))
            copies[n].start()
    norm_rows(x_ref, mod_ref, normed, 0)
    own_heads(normed, w_ref, q_ref, kv, peak_ref, total_ref, acc_ref, 0, lambda n: copies[n].wait())


def own_scratch(tokens, width):
    return [pltpu.VMEM((tokens, width), jnp.bfloat16), pltpu.VMEM((tokens, 2 * INNER), jnp.bfloat16)]


def first_part(x, mod, w):
    tokens, width = x.shape
    state = jax.ShapeDtypeStruct((tokens, INNER), jnp.float32)
    held = [jax.ShapeDtypeStruct(shape, jnp.bfloat16) for shape in [(tokens, INNER), w.shape]]
    return pl.pallas_call(
        first_kernel,
        out_shape=held[:1] + [state] * 3 + held[1:],
        in_specs=[IN_VMEM, IN_VMEM, IN_HBM],
        out_specs=[IN_VMEM] * 5,
        scratch_shapes=own_scratch(tokens, width) + [pltpu.SemaphoreType.DMA((w.shape[1] // (2 * PAIR),))],
        compiler_params=pltpu.CompilerParams(vmem_limit_bytes=FIRST_LIMIT),
        name="first_part",
    )(x, mod, w)


def half_kernel(x_ref, mod_ref, w_ref, qkv_ref, normed):
    norm_rows(x_ref, mod_ref, normed, 0)
    for c in range(0, 3 * INNER, 4 * HD):
        qkv_ref[:, c : c + 4 * HD] = project(normed[...], w_ref, c, 4 * HD)


def half_part(x, mod, w):
    rows, width = x.shape
    return pl.pallas_call(
        half_kernel,
        out_shape=jax.ShapeDtypeStruct((rows, w.shape[1]), jnp.bfloat16),
        in_specs=[IN_VMEM] * 3,
        out_specs=IN_VMEM,
        scratch_shapes=[pltpu.VMEM((rows, width), jnp.bfloat16)],
        compiler_params=pltpu.CompilerParams(vmem_limit_bytes=LIMIT),
        name="half_part",
    )(x, mod, w)


def second_kernel(a_ref, b_ref, qkv_ref, mod_ref, w_ref, x_ref, q_ref, peak_ref, total_ref, acc_ref, normed, kv):
    rows = a_ref.shape[0]
    x_ref[:rows, :] = a_ref[...]
    x_ref[rows:, :] = b_ref[...]
    q_ref[:rows, :] = qkv_ref[:, :INNER]
    kv[:rows, :] = qkv_ref[:, INNER:]
    norm_rows(b_ref, mod_ref, normed, 0)
    own_heads(normed, w_ref, q_ref, kv, peak_ref, total_ref, acc_ref, rows, lambda n: None)


def second_part(a, b, qkv, mod, w):
    tokens, width = a.shape[0] + b.shape[0], a.shape[1]
    state = jax.ShapeDtypeStruct((tokens, INNER), jnp.float32)
    half = [jax.ShapeDtypeStruct(shape, jnp.bfloat16) for shape in ((tokens, width), (tokens, INNER))]
    return pl.pallas_call(
        second_kernel,
        out_shape=half + [state] * 3,
        in_specs=[IN_VMEM] * 5,
        out_specs=[IN_VMEM] * 5,
        scratch_shapes=[
            pltpu.VMEM(b.shape, jnp.bfloat16),
            pltpu.VMEM((tokens, 2 * INNER), jnp.bfloat16),
        ],
        compiler_params=pltpu.CompilerParams(vmem_limit_bytes=LIMIT),
        name="second_part",
    )(a, b, qkv, mod, w)


def uses(key_ref, count_ref, me, owner, blocks_here):
    used = jnp.bool_(False)
    for i in range(blocks_here):
        row = me * blocks_here + i
        for j in range(blocks_here, key_ref.shape[0]):
            used = used | ((key_ref[j, row] // blocks_here == owner) & (j < count_ref[row]))
    return used & (owner != me)


def project_block(block_ref, mod_ref, w_ref, normed, row, kv_ref):
    rows = slice(row, row + BLK)
    norm_rows(block_ref, mod_ref, normed, row)
    for c in range(0, 2 * INNER, 2 * PAIR):
        kv_ref[rows, c : c + 2 * PAIR] = project(normed[rows, :], w_ref, INNER + c, 2 * PAIR)


def arrived_kernel(count, exchanges, blocks_here, key_ref, count_ref, *rest):
    blocks, (mod_ref, w_ref, kv_ref, normed) = rest[: len(exchanges)], rest[len(exchanges) :]
    me = lax.axis_index("seq")
    partners = partners_here(me, count)
    for n, exchange in enumerate(exchanges):

        @pl.when(uses(key_ref, count_ref, me, partners[exchange], blocks_here))
        def _():
            project_block(blocks[n], mod_ref, w_ref, normed, n * BLK, kv_ref)


def arrived_part(count, exchanges, blocks_here, key_blocks, block_counts, blocks, mod, w):
    rows = len(exchanges) * BLK
    return pl.pallas_call(
        functools.partial(arrived_kernel, count, exchanges, blocks_here),
        out_shape=jax.ShapeDtypeStruct((rows, 2 * INNER), jnp.bfloat16),
        in_specs=[IN_SMEM] * 2 + [IN_VMEM] * (len(blocks) + 2),
        out_specs=IN_VMEM,
        scratch_shapes=[pltpu.VMEM((rows, w.shape[0]), jnp.bfloat16)],
        compiler_params=pltpu.CompilerParams(vmem_limit_bytes=LIMIT),
        name="arrived_part",
    )(key_blocks, block_counts, *blocks, mod, w)


def last_kernel(count, early, late, asked, pieces, key_ref, count_ref, *rest):
    early_ref, *rest = rest
    blocks, rest = rest[: len(late)], rest[len(late) :]
    q_ref, peak_ref, total_ref, acc_ref, x_ref, mod_ref, w_ref, wo_ref, *rest = rest
    if pieces == 1:
        y_out, normed, kv, attended, y_ref, sems = rest
        ys, sends, copies = [y_ref], [], []
    else:
        ys, sends, (normed, kv, attended) = rest[:pieces], rest[pieces:-3], rest[-3:]
    me = lax.axis_index("seq")
    tokens = x_ref.shape[0]
    blocks_here = tokens // BLK
    remote = key_ref.shape[0] - blocks_here
    partners = partners_here(me, count)
    slots = early + late
    for n, exchange in enumerate(slots):

        @pl.when(uses(key_ref, count_ref, me, partners[exchange], blocks_here))
        def _():
            if n < len(early):
                kv[n * BLK : (n + 1) * BLK, :] = early_ref[n * BLK : (n + 1) * BLK, :]
            else:
                project_block(blocks[n - len(early)], mod_ref, w_ref, normed, n * BLK, kv)

    starts, bias = [], []
    for i in range(blocks_here):
        row = me * blocks_here + i
        starts.append([])
        bias.append([])
        for j in range(remote):
            live = blocks_here + j < count_ref[row]
            bias[i].append(jnp.where(live, 0.0, MASKED))
            owner = key_ref[blocks_here + j, row] // blocks_here
            owner = jnp.where(live, owner, key_ref[blocks_here, row] // blocks_here)
            start = jnp.int32(0)
            for n, exchange in enumerate(slots):
                start = jnp.where(owner == partners[exchange], n * BLK, start)
            starts[i].append(pl.multiple_of(start, BLK))

    def listed(i, cols):
        return jnp.concatenate([kv[pl.ds(start, BLK), cols] for start in starts[i]], axis=0)

    for at in range(0, INNER, HD):
        here = slice(at, at + HD)
        for i in range(blocks_here):
            rows = slice(i * BLK, (i + 1) * BLK)
            s = scores_of(q_ref[rows, here], listed(i, here))
            s = [s[:, j * BLK : (j + 1) * BLK] + bias[i][j] for j in range(remote)]
            old_peak = peak_ref[rows, here]
            peak = old_peak
            for part in s:
                peak = jnp.maximum(peak, jnp.max(part, axis=-1, keepdims=True))
            p = jnp.concatenate([jnp.exp2((part - peak) * TO_EXP2).astype(jnp.bfloat16) for part in s], axis=1)
            v = with_ones(listed(i, slice(INNER + at, INNER + at + HD)))
            both = jnp.dot(p, v, preferred_element_type=jnp.float32)
            keep = jnp.exp2((old_peak - peak) * TO_EXP2)
            total = total_ref[rows, here] * keep + both[:, HD:]
            acc = acc_ref[rows, here] * keep + both[:, :HD]
            attended[rows, here] = (acc / total).astype(jnp.bfloat16)
    for c in range(0, wo_ref.shape[1], 2 * PAIR):
        cols = slice(c, c + 2 * PAIR)
        out = jnp.dot(attended[...], wo_ref[:, cols], preferred_element_type=jnp.float32)
        y = (x_ref[:, cols].astype(jnp.float32) + mod_ref[2, :, cols] * out).astype(jnp.bfloat16)
        for n, y_ref in enumerate(ys):
            rows = tokens // pieces
            y_ref[:, cols] = y[n * rows : (n + 1) * rows]
        if pieces == 1:
            copies.append(pltpu.make_async_copy(ys[0].at[:, cols], y_out.at[:, cols], sems.at[len(copies)]))
            copies[-1].start()
    send_asked(count, asked, key_ref, ys, sends)
    if pieces == 1:
        for copy in copies:
            copy.wait()


def last_part(count, early, late, asked, pieces, key_blocks, block_counts, early_kv, blocks, q, state, x, mod, w, wo):
    part = jax.ShapeDtypeStruct((BLK, x.shape[1]), x.dtype)
    piece = jax.ShapeDtypeStruct((x.shape[0] // pieces, x.shape[1]), x.dtype)
    slots = len(early) + len(late)
    written = []
    if pieces == 1:
        written = [pltpu.VMEM(x.shape, x.dtype), pltpu.SemaphoreType.DMA((wo.shape[1] // (2 * PAIR),))]
    return pl.pallas_call(
        functools.partial(last_kernel, count, early, late, asked, pieces),
        out_shape=[piece] * pieces + [part] * len(asked),
        in_specs=[IN_SMEM] * 2 + [IN_VMEM] * (9 + len(late)),
        out_specs=[IN_HBM] if pieces == 1 else [IN_VMEM] * (pieces + len(asked)),
        scratch_shapes=[
            pltpu.VMEM((slots * BLK, w.shape[0]), jnp.bfloat16),
            pltpu.VMEM((slots * BLK, 2 * INNER), jnp.bfloat16),
            pltpu.VMEM((x.shape[0], INNER), jnp.bfloat16),
        ]
        + written,
        compiler_params=pltpu.CompilerParams(vmem_limit_bytes=LIMIT),
        name="last_part",
    )(key_blocks, block_counts, early_kv, *blocks, q, *state, x, mod, w, wo)


def on_device(activations, qkv_weight, out_weight, modulation, key_blocks, block_counts):
    count = lax.axis_size("seq")
    sections = lax.axis_size("section")
    x, w, wo = activations[0], qkv_weight[0], out_weight[0]
    mod = modulation.reshape(modulation.shape[1], 1, modulation.shape[2])
    key_blocks = key_blocks.T
    lists_of = (key_blocks, block_counts)
    here = [(s, s) for s in range(sections)]
    onward = [(s, (s + 1) % sections) for s in range(sections)]

    def exchange(send, i, hops):
        pairs = [(s * count + a, t * count + b) for s, t in hops for a, b in pairs_of(i, count)]
        return lax.ppermute(send, ("section", "seq"), pairs)

    order = FIRST_EARLY + FIRST_LATE
    blocks_here = x.shape[0] // BLK
    got = {i: exchange(send, i, here) for i, send in zip(order, pick_blocks([x], key_blocks, count, order))}
    q, *state, w = first_part(x, mod, w)
    early = arrived_part(count, FIRST_EARLY, blocks_here, *lists_of, [got[i] for i in FIRST_EARLY], mod, w)
    blocks = [got[i] for i in FIRST_LATE]
    made = last_part(
        count, FIRST_EARLY, FIRST_LATE, SWAPPED, PIECES, *lists_of, early, blocks, q, state, x, mod, w, wo
    )
    pieces, sends = made[:PIECES], made[PIECES:]

    pieces = [lax.ppermute(piece, "section", onward) for piece in pieces]
    swapped = [exchange(send, i, here) for i, send in zip(SWAPPED, sends)]
    got = {i: lax.ppermute(block, "section", onward) for i, block in zip(SWAPPED, swapped)}
    qkv = half_part(pieces[0], mod, w)
    pieces[1], qkv = lax.optimization_barrier((pieces[1], qkv))
    relayed = tuple(i for i in order if i not in SWAPPED)
    params = pltpu.CompilerParams(vmem_limit_bytes=LIMIT)
    sends = pick_blocks(pieces, key_blocks, count, relayed, params)
    got.update({i: exchange(send, i, here) for i, send in zip(relayed, sends)})
    x, q, *state = second_part(*pieces, qkv, mod, w)
    early = arrived_part(count, SECOND_EARLY, blocks_here, *lists_of, [got[i] for i in SECOND_EARLY], mod, w)
    blocks = [got[i] for i in SECOND_LATE]
    (out,) = last_part(
        count, SECOND_EARLY, SECOND_LATE, (), 1, *lists_of, early, blocks, q, state, x, mod, w, wo
    )
    return out[None]


def solution(mesh):
    return jax.shard_map(
        on_device,
        mesh=mesh,
        in_specs=(
            P("section", "seq", None),
            P("section", None, None),
            P("section", None, None),
            P("section", None, None),
            P(),
            P(),
        ),
        out_specs=P("section", "seq", None),
        check_vma=False,
    )
```

profile of v0, /device:TPU:8, one launch (start us, length us, event | category | flops | bytes accessed | tf_op | source)
XLA Modules:
  0.0 68.7 jit_solution(1320181455197308541)
XLA Ops:
  0.0 2.4 %pick_blocks.2 = (bf16[128,1536]{1,0:T(8,128)(2,1)}, bf16[128,1536]{1,0:T(8,128)(2,1)}, bf16[128,1536]{1,0:T(8,128)(2,1)}, bf16[128,1536]{1,0:T(8,128)(2,1)}) custom-call(s32[4,16]{1,0:T(4,128)} %bitcast.20, bf16[256,1536]{1,0:T(8,128)(2,1)} %bitcast.10), custom_call_target="tpu_custom_call" | custom-call | tf_op jit(solution)/shard_map/pick_blocks/pallas_call | solution.py:74
  2.4 3.3 %collective-permute-start = (bf16[128,1536]{1,0:T(8,128)(2,1)}, bf16[128,1536]{1,0:T(8,128)(2,1)S(1)}, u32[]{:S(2)}, u32[]{:S(2)}) collective-permute-start(bf16[128,1536]{1,0:T(8,128)(2,1)} %get-tuple-element.27), channel_id=1, source_target_pairs={{0,0},{1,2},{2,1},{3,4},{4,3},{5,6},{6,5},{7,7},{8,8},{9,10},{10,9... | collective-permute-start | bytes 1179656 | tf_op jit(solution)/shard_map/ppermute | solution.py:388
  5.7 1.7 %collective-permute-start.1 = (bf16[128,1536]{1,0:T(8,128)(2,1)}, bf16[128,1536]{1,0:T(8,128)(2,1)S(1)}, u32[]{:S(2)}, u32[]{:S(2)}) collective-permute-start(bf16[128,1536]{1,0:T(8,128)(2,1)} %get-tuple-element.29), channel_id=1, source_target_pairs={{0,1},{1,0},{2,3},{3,2},{4,5},{5,4},{6,7},{7,6},{8,9},{9,8},{10,11... | collective-permute-start | bytes 1179656 | tf_op jit(solution)/shard_map/ppermute | solution.py:388
  7.4 0.4 collective-permute-start.2
  7.9 3.0 %collective-permute-start.3 = (bf16[128,1536]{1,0:T(8,128)(2,1)}, bf16[128,1536]{1,0:T(8,128)(2,1)S(1)}, u32[]{:S(2)}, u32[]{:S(2)}) collective-permute-start(bf16[128,1536]{1,0:T(8,128)(2,1)} %get-tuple-element.31), channel_id=1, source_target_pairs={{0,0},{1,1},{2,4},{3,5},{4,2},{5,3},{6,6},{7,7},{8,8},{9,9},{10,12... | collective-permute-start | bytes 1179656 | tf_op jit(solution)/shard_map/ppermute | solution.py:388
  10.9 0.0 copy-start
  10.9 1.1 %copy-done = bf16[1,256,1536]{2,1,0:T(8,128)(2,1)S(1)} copy-done((bf16[1,256,1536]{2,1,0:T(8,128)(2,1)S(1)}, bf16[1,256,1536]{2,1,0:T(8,128)(2,1)}, u32[]{:S(2)}) %copy-start) | copy-done | bytes 786456
  12.1 0.0 copy-start.2
  12.1 0.7 %copy-done.2 = f32[1,3,1536]{2,0,1:T(1,128)S(1)} copy-done((f32[1,3,1536]{2,0,1:T(1,128)S(1)}, f32[1,3,1536]{2,0,1:T(1,128)}, u32[]{:S(2)}) %copy-start.2) | copy-done | bytes 18456
  12.8 0.0 copy-start.4
  12.8 0.0 copy-start.5
  12.8 8.3 %first_part.1 = (bf16[256,1536]{1,0:T(8,128)(2,1)S(1)}, f32[256,1536]{1,0:T(8,128)S(1)}, f32[256,1536]{1,0:T(8,128)S(1)}, f32[256,1536]{1,0:T(8,128)S(1)}, bf16[1536,4608]{1,0:T(8,128)(2,1)S(1)}) custom-call(bf16[256,1536]{1,0:T(8,128)(2,1)S(1)} %bitcast.11, f32[3,1,1536]{2,1,0:T(1,128)S(1)} %bitcast.13, bf16[1536,4608]{1,0:T(8,128)(2,1)} %bitcast.26), custom_call_target="tpu_custom_call" | custom-call | tf_op jit(solution)/shard_map/first_part/pallas_call | solution.py:180
  21.1 0.0 collective-permute-done.rest_0_
  21.1 0.0 slice-start
  21.1 0.0 copy-done.4
  21.1 0.0 copy-done.5
  21.1 0.0 slice-start.1
  21.1 0.0 copy-start.1
  21.1 2.3 %arrived_part.2.rest_0_ = bf16[128,3072]{1,0:T(8,128)(2,1)S(1)} custom-call(s32[4,16]{1,0:T(4,128)S(1)} %bitcast.21, s32[16]{0:T(128)S(1)} %copy-done.5, bf16[128,1536]{1,0:T(8,128)(2,1)S(1)} %collective-permute-done.rest_0_, f32[3,1,1536]{2,1,0:T(1,128)S(1)} %bitcast.14, bf16[1536,4608]{1,0:T(8,128)(2,1)S(1)} %get-tuple-element.28.rest_2_.rest_10_.w_ref.rest_4_.rest_8_), custom_call_target="tpu_custom_call" | custom-call | tf_op jit(solution)/shard_map/arrived_part/pallas_call | solution.py:267
  23.4 1.3 %collective-permute-done.1.rest_1_ = bf16[128,1536]{1,0:T(8,128)(2,1)S(1)} collective-permute-done((bf16[128,1536]{1,0:T(8,128)(2,1)}, bf16[128,1536]{1,0:T(8,128)(2,1)S(1)}, u32[]{:S(2)}, u32[]{:S(2)}) %collective-permute-start.1) | collective-permute-done | bytes 393248 | tf_op jit(solution)/shard_map/ppermute | solution.py:388
  24.7 0.0 collective-permute-done.2.rest_2_
  24.7 0.1 collective-permute-done.3.rest_3_
  24.8 0.0 slice-done
  24.8 0.0 slice-done.1
  24.8 0.0 copy-done.1
  24.8 0.0 copy-start.3
  24.8 7.7 %last_part.2 = (bf16[128,1536]{1,0:T(8,128)(2,1)S(1)}, bf16[128,1536]{1,0:T(8,128)(2,1)S(1)}, bf16[128,1536]{1,0:T(8,128)(2,1)S(1)}) custom-call(s32[4,16]{1,0:T(4,128)S(1)} %bitcast.22, s32[16]{0:T(128)S(1)} %copy-done.5, bf16[128,3072]{1,0:T(8,128)(2,1)S(1)} %arrived_part.2.rest_0_, bf16[128,1536]{1,0:T(8,128)(2,1)S(1)} %collective-permute-done.1.rest_1_, ...), custom_call_target="tpu_custom_call" | custom-call | tf_op jit(solution)/shard_map/last_part/pallas_call | solution.py:360
  32.5 0.1 collective-permute-start.4
  32.6 1.6 %collective-permute-start.5 = (bf16[128,1536]{1,0:T(8,128)(2,1)S(1)}, bf16[128,1536]{1,0:T(8,128)(2,1)S(1)}, u32[]{:S(2)}, u32[]{:S(2)}) collective-permute-start(bf16[128,1536]{1,0:T(8,128)(2,1)S(1)} %get-tuple-element.37), channel_id=1, source_target_pairs={{0,8},{8,16},{16,24},{24,0},{1,9},{9,17},{17,25},{25,1},{2,10},{10... | collective-permute-start | bytes 1179656 | tf_op jit(solution)/shard_map/ppermute | solution.py:401
  34.2 1.9 %collective-permute-start.8 = (bf16[128,1536]{1,0:T(8,128)(2,1)S(1)}, bf16[128,1536]{1,0:T(8,128)(2,1)S(1)}, u32[]{:S(2)}, u32[]{:S(2)}) collective-permute-start(bf16[128,1536]{1,0:T(8,128)(2,1)S(1)} %get-tuple-element.41), channel_id=1, source_target_pairs={{0,0},{1,2},{2,1},{3,4},{4,3},{5,6},{6,5},{7,7},{8,8},{9,10},{10,9... | collective-permute-start | bytes 1179656 | tf_op jit(solution)/shard_map/ppermute | solution.py:388
  36.1 3.7 %collective-permute-done.4.x_ref.refs_0_.a_ref = bf16[128,1536]{1,0:T(8,128)(2,1)S(1)} collective-permute-done((bf16[128,1536]{1,0:T(8,128)(2,1)S(1)}, bf16[128,1536]{1,0:T(8,128)(2,1)S(1)}, u32[]{:S(2)}, u32[]{:S(2)}) %collective-permute-start.4) | collective-permute-done | bytes 393248 | tf_op jit(solution)/shard_map/ppermute | solution.py:401
  39.8 0.0 copy-done.3
  39.8 2.3 %half_part.1.qkv_ref = bf16[128,4608]{1,0:T(8,128)(2,1)S(1)} custom-call(bf16[128,1536]{1,0:T(8,128)(2,1)S(1)} %collective-permute-done.4.x_ref.refs_0_.a_ref, f32[3,1,1536]{2,1,0:T(1,128)S(1)} %bitcast.16, bf16[1536,4608]{1,0:T(8,128)(2,1)S(1)} %get-tuple-element.28.rest_2_.rest_10_.w_ref.rest_4_.rest_8_), custom_call_target="tpu_custom_call" | custom-call | tf_op jit(solution)/shard_map/half_part/pallas_call | solution.py:199
  42.1 1.9 %collective-permute-done.5.refs_1_.b_ref = bf16[128,1536]{1,0:T(8,128)(2,1)S(1)} collective-permute-done((bf16[128,1536]{1,0:T(8,128)(2,1)S(1)}, bf16[128,1536]{1,0:T(8,128)(2,1)S(1)}, u32[]{:S(2)}, u32[]{:S(2)}) %collective-permute-start.5) | collective-permute-done | bytes 393248 | tf_op jit(solution)/shard_map/ppermute | solution.py:401
  44.0 0.7 %pick_blocks.3 = (bf16[128,1536]{1,0:T(8,128)(2,1)S(1)}, bf16[128,1536]{1,0:T(8,128)(2,1)S(1)}, bf16[128,1536]{1,0:T(8,128)(2,1)S(1)}) custom-call(s32[4,16]{1,0:T(4,128)S(1)} %bitcast.23, bf16[128,1536]{1,0:T(8,128)(2,1)S(1)} %collective-permute-done.4.x_ref.refs_0_.a_ref, bf16[128,1536]{1,0:T(8,128)(2,1)S(1)} %collective-permute-done.5.refs_1_.b_ref), custom_call_target="tpu_custom_call" | custom-call | tf_op jit(solution)/shard_map/pick_blocks/pallas_call | solution.py:74
  44.7 3.2 %collective-permute-start.6 = (bf16[128,1536]{1,0:T(8,128)(2,1)S(1)}, bf16[128,1536]{1,0:T(8,128)(2,1)S(1)}, u32[]{:S(2)}, u32[]{:S(2)}) collective-permute-start(bf16[128,1536]{1,0:T(8,128)(2,1)S(1)} %get-tuple-element.39), channel_id=1, source_target_pairs={{0,1},{1,0},{2,3},{3,2},{4,5},{5,4},{6,7},{7,6},{8,9},{9,8},{10,11... | collective-permute-start | bytes 1179656 | tf_op jit(solution)/shard_map/ppermute | solution.py:388
  47.9 0.0 collective-permute-start.7
  47.9 0.2 collective-permute-done.8
  48.0 0.0 collective-permute-start.9
  48.1 3.9 %collective-permute-start.10 = (bf16[128,1536]{1,0:T(8,128)(2,1)S(1)}, bf16[128,1536]{1,0:T(8,128)(2,1)S(1)}, u32[]{:S(2)}, u32[]{:S(2)}) collective-permute-start(bf16[128,1536]{1,0:T(8,128)(2,1)S(1)} %get-tuple-element.42), channel_id=1, source_target_pairs={{0,0},{1,1},{2,4},{3,5},{4,2},{5,3},{6,6},{7,7},{8,8},{9,9},{10,12... | collective-permute-start | bytes 1179656 | tf_op jit(solution)/shard_map/ppermute | solution.py:388
  52.0 3.5 %second_part.1 = (bf16[256,1536]{1,0:T(8,128)(2,1)S(1)}, bf16[256,1536]{1,0:T(8,128)(2,1)S(1)}, f32[256,1536]{1,0:T(8,128)S(1)}, f32[256,1536]{1,0:T(8,128)S(1)}, f32[256,1536]{1,0:T(8,128)S(1)}) custom-call(bf16[128,1536]{1,0:T(8,128)(2,1)S(1)} %collective-permute-done.4.x_ref.refs_0_.a_ref, bf16[128,1536]{1,0:T(8,128)(2,1)S(1)} %collective-permute-done.5.refs_1_.b_ref, ...), custom_call_target="tpu_custom_call" | custom-call | tf_op jit(solution)/shard_map/second_part/pallas_call | solution.py:224
  55.5 1.6 %collective-permute-done.6.rest_0_ = bf16[128,1536]{1,0:T(8,128)(2,1)S(1)} collective-permute-done((bf16[128,1536]{1,0:T(8,128)(2,1)S(1)}, bf16[128,1536]{1,0:T(8,128)(2,1)S(1)}, u32[]{:S(2)}, u32[]{:S(2)}) %collective-permute-start.6) | collective-permute-done | bytes 393248 | tf_op jit(solution)/shard_map/ppermute | solution.py:388
  57.1 0.7 collective-permute-done.7.rest_1_
  57.8 0.0 collective-permute-done.9.rest_2_
  57.8 4.2 %arrived_part.3.rest_0_ = bf16[384,3072]{1,0:T(8,128)(2,1)S(1)} custom-call(s32[4,16]{1,0:T(4,128)S(1)} %bitcast.24, s32[16]{0:T(128)S(1)} %copy-done.5, bf16[128,1536]{1,0:T(8,128)(2,1)S(1)} %collective-permute-done.6.rest_0_, bf16[128,1536]{1,0:T(8,128)(2,1)S(1)} %collective-permute-done.7.rest_1_, bf16[128,1536]{1,0:T(8,128)(2,1)S(1)} %collective-permute-done.9.rest_2_, ...), custom_call_target="tpu_custom_call" | custom-call | tf_op jit(solution)/shard_map/arrived_part/pallas_call | solution.py:267
  62.0 0.0 collective-permute-done.10.rest_1_
  62.0 6.5 %last_part.3 = bf16[256,1536]{1,0:T(8,128)(2,1)} custom-call(s32[4,16]{1,0:T(4,128)S(1)} %bitcast.25, s32[16]{0:T(128)S(1)} %copy-done.5, bf16[384,3072]{1,0:T(8,128)(2,1)S(1)} %arrived_part.3.rest_0_, bf16[128,1536]{1,0:T(8,128)(2,1)S(1)} %collective-permute-done.10.rest_1_, bf16[256,1536]{1,0:T(8,128)(2,1)S(1)} %get-tuple-element.44.rest_2_, ...), custom_call_target="tpu_custom_call" | custom-call | tf_op jit(solution)/shard_map/last_part/pallas_call | solution.py:360
  (1 shorter events, 0.0 us)
Async XLA Ops:
  2.4 18.7 %collective-permute-start = (bf16[128,1536]{1,0:T(8,128)(2,1)}, bf16[128,1536]{1,0:T(8,128)(2,1)S(1)}, u32[]{:S(2)}, u32[]{:S(2)}) collective-permute-start(bf16[128,1536]{1,0:T(8,128)(2,1)} %get-tuple-element.27), channel_id=1, source_target_pairs={{0,0},{1,2},{2,1},{3,4},{4,3},{5,6},{6,5},{7,7},{8,8},{9,10},{10,9... | collective-permute-start | bytes 1179656 | tf_op jit(solution)/shard_map/ppermute | solution.py:388
  5.7 19.0 %collective-permute-start.1 = (bf16[128,1536]{1,0:T(8,128)(2,1)}, bf16[128,1536]{1,0:T(8,128)(2,1)S(1)}, u32[]{:S(2)}, u32[]{:S(2)}) collective-permute-start(bf16[128,1536]{1,0:T(8,128)(2,1)} %get-tuple-element.29), channel_id=1, source_target_pairs={{0,1},{1,0},{2,3},{3,2},{4,5},{5,4},{6,7},{7,6},{8,9},{9,8},{10,11... | collective-permute-start | bytes 1179656 | tf_op jit(solution)/shard_map/ppermute | solution.py:388
  7.4 17.3 %collective-permute-start.2 = (bf16[128,1536]{1,0:T(8,128)(2,1)}, bf16[128,1536]{1,0:T(8,128)(2,1)S(1)}, u32[]{:S(2)}, u32[]{:S(2)}) collective-permute-start(bf16[128,1536]{1,0:T(8,128)(2,1)} %get-tuple-element.30), channel_id=1, source_target_pairs={{0,2},{1,3},{2,0},{3,1},{4,6},{5,7},{6,4},{7,5},{8,10},{9,11},{10,... | collective-permute-start | bytes 1179656 | tf_op jit(solution)/shard_map/ppermute | solution.py:388
  7.9 16.9 %collective-permute-start.3 = (bf16[128,1536]{1,0:T(8,128)(2,1)}, bf16[128,1536]{1,0:T(8,128)(2,1)S(1)}, u32[]{:S(2)}, u32[]{:S(2)}) collective-permute-start(bf16[128,1536]{1,0:T(8,128)(2,1)} %get-tuple-element.31), channel_id=1, source_target_pairs={{0,0},{1,1},{2,4},{3,5},{4,2},{5,3},{6,6},{7,7},{8,8},{9,9},{10,12... | collective-permute-start | bytes 1179656 | tf_op jit(solution)/shard_map/ppermute | solution.py:388
  10.9 1.1 %copy-start = (bf16[1,256,1536]{2,1,0:T(8,128)(2,1)S(1)}, bf16[1,256,1536]{2,1,0:T(8,128)(2,1)}, u32[]{:S(2)}) copy-start(bf16[1,256,1536]{2,1,0:T(8,128)(2,1)} %param.6) | copy-start | bytes 2359300
  12.1 0.7 %copy-start.2 = (f32[1,3,1536]{2,0,1:T(1,128)S(1)}, f32[1,3,1536]{2,0,1:T(1,128)}, u32[]{:S(2)}) copy-start(f32[1,3,1536]{2,0,1:T(1,128)} %param.9) | copy-start | bytes 55300
  12.8 8.3 %copy-start.4 = (s32[16,4]{0,1:T(4,128)S(1)}, s32[16,4]{0,1:T(4,128)}, u32[]{:S(2)}) copy-start(s32[16,4]{0,1:T(4,128)} %param.10) | copy-start | bytes 772
  12.8 8.3 %copy-start.5 = (s32[16]{0:T(128)S(1)}, s32[16]{0:T(128)}, u32[]{:S(2)}) copy-start(s32[16]{0:T(128)} %count_ref.7) | copy-start | bytes 196
  21.1 3.7 %slice-start = ((s8[4718592]{0:T(1024)(128)(4,1)}), s8[4194304]{0:T(1024)(128)(4,1)S(1)}, s32[]{:S(2)}) async-start(s8[4718592]{0:T(1024)(128)(4,1)} %bitcast.6), calls=%async_computation | async-start | bytes 8388608
  21.1 3.7 %slice-start.1 = ((s8[4718592]{0:T(1024)(128)(4,1)}), s8[524288]{0:T(1024)(128)(4,1)S(1)}, s32[]{:S(2)}) async-start(s8[4718592]{0:T(1024)(128)(4,1)} %bitcast.6), calls=%async_computation.1 | async-start | bytes 1048576
  21.1 3.7 %copy-start.1 = (bf16[1,256,1536]{2,1,0:T(8,128)(2,1)S(1)}, bf16[1,256,1536]{2,1,0:T(8,128)(2,1)}, u32[]{:S(2)}) copy-start(bf16[1,256,1536]{2,1,0:T(8,128)(2,1)} %param.6) | copy-start | bytes 2359300
  24.8 15.0 %copy-start.3 = (f32[1,3,1536]{2,0,1:T(1,128)S(1)}, f32[1,3,1536]{2,0,1:T(1,128)}, u32[]{:S(2)}) copy-start(f32[1,3,1536]{2,0,1:T(1,128)} %param.9) | copy-start | bytes 55300
  32.5 7.3 %collective-permute-start.4 = (bf16[128,1536]{1,0:T(8,128)(2,1)S(1)}, bf16[128,1536]{1,0:T(8,128)(2,1)S(1)}, u32[]{:S(2)}, u32[]{:S(2)}) collective-permute-start(bf16[128,1536]{1,0:T(8,128)(2,1)S(1)} %get-tuple-element.36), channel_id=1, source_target_pairs={{0,8},{8,16},{16,24},{24,0},{1,9},{9,17},{17,25},{25,1},{2,10},{10... | collective-permute-start | bytes 1179656 | tf_op jit(solution)/shard_map/ppermute | solution.py:401
  32.6 11.4 %collective-permute-start.5 = (bf16[128,1536]{1,0:T(8,128)(2,1)S(1)}, bf16[128,1536]{1,0:T(8,128)(2,1)S(1)}, u32[]{:S(2)}, u32[]{:S(2)}) collective-permute-start(bf16[128,1536]{1,0:T(8,128)(2,1)S(1)} %get-tuple-element.37), channel_id=1, source_target_pairs={{0,8},{8,16},{16,24},{24,0},{1,9},{9,17},{17,25},{25,1},{2,10},{10... | collective-permute-start | bytes 1179656 | tf_op jit(solution)/shard_map/ppermute | solution.py:401
  34.2 13.9 %collective-permute-start.8 = (bf16[128,1536]{1,0:T(8,128)(2,1)S(1)}, bf16[128,1536]{1,0:T(8,128)(2,1)S(1)}, u32[]{:S(2)}, u32[]{:S(2)}) collective-permute-start(bf16[128,1536]{1,0:T(8,128)(2,1)S(1)} %get-tuple-element.41), channel_id=1, source_target_pairs={{0,0},{1,2},{2,1},{3,4},{4,3},{5,6},{6,5},{7,7},{8,8},{9,10},{10,9... | collective-permute-start | bytes 1179656 | tf_op jit(solution)/shard_map/ppermute | solution.py:388
  44.7 12.3 %collective-permute-start.6 = (bf16[128,1536]{1,0:T(8,128)(2,1)S(1)}, bf16[128,1536]{1,0:T(8,128)(2,1)S(1)}, u32[]{:S(2)}, u32[]{:S(2)}) collective-permute-start(bf16[128,1536]{1,0:T(8,128)(2,1)S(1)} %get-tuple-element.39), channel_id=1, source_target_pairs={{0,1},{1,0},{2,3},{3,2},{4,5},{5,4},{6,7},{7,6},{8,9},{9,8},{10,11... | collective-permute-start | bytes 1179656 | tf_op jit(solution)/shard_map/ppermute | solution.py:388
  47.9 9.9 %collective-permute-start.7 = (bf16[128,1536]{1,0:T(8,128)(2,1)S(1)}, bf16[128,1536]{1,0:T(8,128)(2,1)S(1)}, u32[]{:S(2)}, u32[]{:S(2)}) collective-permute-start(bf16[128,1536]{1,0:T(8,128)(2,1)S(1)} %get-tuple-element.40), channel_id=1, source_target_pairs={{0,2},{1,3},{2,0},{3,1},{4,6},{5,7},{6,4},{7,5},{8,10},{9,11},{10,... | collective-permute-start | bytes 1179656 | tf_op jit(solution)/shard_map/ppermute | solution.py:388
  48.0 9.7 %collective-permute-start.9 = (bf16[128,1536]{1,0:T(8,128)(2,1)S(1)}, bf16[128,1536]{1,0:T(8,128)(2,1)S(1)}, u32[]{:S(2)}, u32[]{:S(2)}) collective-permute-start(bf16[128,1536]{1,0:T(8,128)(2,1)S(1)} %collective-permute-done.8), channel_id=1, source_target_pairs={{0,8},{8,16},{16,24},{24,0},{1,9},{9,17},{17,25},{25,1},{2,10},{10... | collective-permute-start | bytes 1179656 | tf_op jit(solution)/shard_map/ppermute | solution.py:403
  48.1 13.9 %collective-permute-start.10 = (bf16[128,1536]{1,0:T(8,128)(2,1)S(1)}, bf16[128,1536]{1,0:T(8,128)(2,1)S(1)}, u32[]{:S(2)}, u32[]{:S(2)}) collective-permute-start(bf16[128,1536]{1,0:T(8,128)(2,1)S(1)} %get-tuple-element.42), channel_id=1, source_target_pairs={{0,0},{1,1},{2,4},{3,5},{4,2},{5,3},{6,6},{7,7},{8,8},{9,9},{10,12... | collective-permute-start | bytes 1179656 | tf_op jit(solution)/shard_map/ppermute | solution.py:388
where the time goes:
time: 69.6 us; the launch traced here: 68.7 us
  Pallas kernels  38 us (55%)
  starting transfers between devices  19.1 us (27%)
  waiting for transfers between devices  9.37 us (13%)
  local copies, waits for them, and re-layouts  1.88 us (3%)
    ppermute x8, starting transfers between devices, exchange(): return lax.ppermute(send, ('section', 'seq'), pairs)  17.5 us
    pallas_call x2, Pallas kernels, last_part(): pl.pallas_call(functools.partial(last_kernel, count, early, late, asked,...  14.2 us
    pallas_call x1, Pallas kernels, first_part(): pl.pallas_call(first_kernel, out_shape=held[:1] + [state] * 3 + held[1:],...  8.27 us
    pallas_call x2, Pallas kernels, arrived_part(): pl.pallas_call(functools.partial(arrived_kernel, count, exchanges, blocks...  6.5 us
    ppermute x2, waiting for transfers between devices, on_device(): pieces = [lax.ppermute(piece, 'section', onward) for piece in pieces]  5.6 us
    ppermute x8, waiting for transfers between devices, exchange(): return lax.ppermute(send, ('section', 'seq'), pairs)  3.77 us
    pallas_call x1, Pallas kernels, second_part(): pl.pallas_call(second_kernel, out_shape=half + [state] * 3, in_specs=[IN_...  3.54 us
    pallas_call x2, Pallas kernels, pick_blocks(): pl.pallas_call(functools.partial(pick_kernel, count, exchanges, len(parts...  3.17 us
  transfers between devices with their start and end apart: 11, of which 7 were waited for; matrix products, arithmetic and copies ran while one was open for 0% of the time, Pallas kernels for 31%

commit v1 on v0

--- a/solution.py
+++ b/solution.py
@@ -317,33 +317,44 @@
     def listed(i, cols):
         return jnp.concatenate([kv[pl.ds(start, BLK), cols] for start in starts[i]], axis=0)
 
-    for at in range(0, INNER, HD):
+    def attend(i, at):
         here = slice(at, at + HD)
-        for i in range(blocks_here):
-            rows = slice(i * BLK, (i + 1) * BLK)
-            s = scores_of(q_ref[rows, here], listed(i, here))
-            s = [s[:, j * BLK : (j + 1) * BLK] + bias[i][j] for j in range(remote)]
-            old_peak = peak_ref[rows, here]
-            peak = old_peak
-            for part in s:
-                peak = jnp.maximum(peak, jnp.max(part, axis=-1, keepdims=True))
-            p = jnp.concatenate([jnp.exp2((part - peak) * TO_EXP2).astype(jnp.bfloat16) for part in s], axis=1)
-            v = with_ones(listed(i, slice(INNER + at, INNER + at + HD)))
-            both = jnp.dot(p, v, preferred_element_type=jnp.float32)
-            keep = jnp.exp2((old_peak - peak) * TO_EXP2)
-            total = total_ref[rows, here] * keep + both[:, HD:]
-            acc = acc_ref[rows, here] * keep + both[:, :HD]
-            attended[rows, here] = (acc / total).astype(jnp.bfloat16)
-    for c in range(0, wo_ref.shape[1], 2 * PAIR):
+        rows = slice(i * BLK, (i + 1) * BLK)
+        s = scores_of(q_ref[rows, here], listed(i, here))
+        s = [s[:, j * BLK : (j + 1) * BLK] + bias[i][j] for j in range(remote)]
+        old_peak = peak_ref[rows, here]
+        peak = old_peak
+        for part in s:
+            peak = jnp.maximum(peak, jnp.max(part, axis=-1, keepdims=True))
+        p = jnp.concatenate([jnp.exp2((part - peak) * TO_EXP2).astype(jnp.bfloat16) for part in s], axis=1)
+        v = with_ones(listed(i, slice(INNER + at, INNER + at + HD)))
+        both = jnp.dot(p, v, preferred_element_type=jnp.float32)
+        keep = jnp.exp2((old_peak - peak) * TO_EXP2)
+        total = total_ref[rows, here] * keep + both[:, HD:]
+        acc = acc_ref[rows, here] * keep + both[:, :HD]
+        attended[rows, here] = (acc / total).astype(jnp.bfloat16)
+
+    def write(i, c):
         cols = slice(c, c + 2 * PAIR)
-        out = jnp.dot(attended[...], wo_ref[:, cols], preferred_element_type=jnp.float32)
-        y = (x_ref[:, cols].astype(jnp.float32) + mod_ref[2, :, cols] * out).astype(jnp.bfloat16)
-        for n, y_ref in enumerate(ys):
-            rows = tokens // pieces
-            y_ref[:, cols] = y[n * rows : (n + 1) * rows]
+        rows = slice(i * BLK, (i + 1) * BLK)
+        out = jnp.dot(attended[rows, :], wo_ref[:, cols], preferred_element_type=jnp.float32)
+        y = (x_ref[rows, cols].astype(jnp.float32) + mod_ref[2, :, cols] * out).astype(jnp.bfloat16)
+        each = tokens // pieces
+        at = i * BLK % each
+        ys[i * BLK // each][at : at + BLK, cols] = y
         if pieces == 1:
-            copies.append(pltpu.make_async_copy(ys[0].at[:, cols], y_out.at[:, cols], sems.at[len(copies)]))
+            copies.append(pltpu.make_async_copy(ys[0].at[rows, cols], y_out.at[rows, cols], sems.at[len(copies)]))
             copies[-1].start()
+
+    waiting = []
+    for i in range(blocks_here):
+        for h in range(HEADS):
+            attend(i, h * HD)
+            if waiting and h % 4 == 3:
+                write(*waiting.pop(0))
+        waiting += [(i, c) for c in range(0, wo_ref.shape[1], 2 * PAIR)]
+    for item in waiting:
+        write(*item)
     send_asked(count, asked, key_ref, ys, sends)
     if pieces == 1:
         for copy in copies:
@@ -356,7 +367,7 @@
     slots = len(early) + len(late)
     written = []
     if pieces == 1:
-        written = [pltpu.VMEM(x.shape, x.dtype), pltpu.SemaphoreType.DMA((wo.shape[1] // (2 * PAIR),))]
+        written = [pltpu.VMEM(x.shape, x.dtype), pltpu.SemaphoreType.DMA((wo.shape[1] // (2 * PAIR) * (x.shape[0] // BLK),))]
     return pl.pallas_call(
         functools.partial(last_kernel, count, early, late, asked, pieces),
         out_shape=[piece] * pieces + [part] * len(asked),

time: 69.6 us -> 69.1 us (level)
  the two profiles are of different devices: /device:TPU:8 before, /device:TPU:12 now
where the time goes in v1:
time: 69.1 us; the launch traced here: 69.6 us
  Pallas kernels  37.6 us (54%)
  waiting for transfers between devices  15.1 us (22%)
  starting transfers between devices  14.6 us (21%)
  local copies, waits for them, and re-layouts  1.88 us (3%)
    pallas_call x2, Pallas kernels, last_part(): pl.pallas_call(functools.partial(last_kernel, count, early, late, asked,...  15.5 us
    ppermute x8, starting transfers between devices, exchange(): return lax.ppermute(send, ('section', 'seq'), pairs)  13 us
    ppermute x8, waiting for transfers between devices, exchange(): return lax.ppermute(send, ('section', 'seq'), pairs)  9.54 us
    pallas_call x1, Pallas kernels, first_part(): pl.pallas_call(first_kernel, out_shape=held[:1] + [state] * 3 + held[1:],...  8.27 us
    ppermute x2, waiting for transfers between devices, on_device(): pieces = [lax.ppermute(piece, 'section', onward) for piece in pieces]  5.6 us
    pallas_call x2, Pallas kernels, arrived_part(): pl.pallas_call(functools.partial(arrived_kernel, count, exchanges, blocks...  4.84 us
    pallas_call x1, Pallas kernels, second_part(): pl.pallas_call(second_kernel, out_shape=half + [state] * 3, in_specs=[IN_...  3.54 us
    pallas_call x2, Pallas kernels, pick_blocks(): pl.pallas_call(functools.partial(pick_kernel, count, exchanges, len(parts...  3.17 us
  transfers between devices with their start and end apart: 11, of which 6 were waited for; matrix products, arithmetic and copies ran while one was open for 0% of the time, Pallas kernels for 28%

profile of v1, /device:TPU:12, one launch (start us, length us, event | category | flops | bytes accessed | tf_op | source)
XLA Modules:
  0.0 69.6 jit_solution(7781772649969214771)
XLA Ops:
  0.0 2.4 %pick_blocks.2 = (bf16[128,1536]{1,0:T(8,128)(2,1)}, bf16[128,1536]{1,0:T(8,128)(2,1)}, bf16[128,1536]{1,0:T(8,128)(2,1)}, bf16[128,1536]{1,0:T(8,128)(2,1)}) custom-call(s32[4,16]{1,0:T(4,128)} %bitcast.20, bf16[256,1536]{1,0:T(8,128)(2,1)} %bitcast.10), custom_call_target="tpu_custom_call" | custom-call | tf_op jit(solution)/shard_map/pick_blocks/pallas_call | solution.py:74
  2.4 3.4 %collective-permute-start = (bf16[128,1536]{1,0:T(8,128)(2,1)}, bf16[128,1536]{1,0:T(8,128)(2,1)S(1)}, u32[]{:S(2)}, u32[]{:S(2)}) collective-permute-start(bf16[128,1536]{1,0:T(8,128)(2,1)} %get-tuple-element.27), channel_id=1, source_target_pairs={{0,0},{1,2},{2,1},{3,4},{4,3},{5,6},{6,5},{7,7},{8,8},{9,10},{10,9... | collective-permute-start | bytes 1179656 | tf_op jit(solution)/shard_map/ppermute | solution.py:399
  5.8 0.5 collective-permute-start.1
  6.3 0.1 collective-permute-start.2
  6.4 4.9 %collective-permute-start.3 = (bf16[128,1536]{1,0:T(8,128)(2,1)}, bf16[128,1536]{1,0:T(8,128)(2,1)S(1)}, u32[]{:S(2)}, u32[]{:S(2)}) collective-permute-start(bf16[128,1536]{1,0:T(8,128)(2,1)} %get-tuple-element.31), channel_id=1, source_target_pairs={{0,0},{1,1},{2,4},{3,5},{4,2},{5,3},{6,6},{7,7},{8,8},{9,9},{10,12... | collective-permute-start | bytes 1179656 | tf_op jit(solution)/shard_map/ppermute | solution.py:399
  11.4 0.0 copy-start
  11.4 1.1 %copy-done = bf16[1,256,1536]{2,1,0:T(8,128)(2,1)S(1)} copy-done((bf16[1,256,1536]{2,1,0:T(8,128)(2,1)S(1)}, bf16[1,256,1536]{2,1,0:T(8,128)(2,1)}, u32[]{:S(2)}) %copy-start) | copy-done | bytes 786456
  12.5 0.0 copy-start.2
  12.5 0.7 %copy-done.2 = f32[1,3,1536]{2,0,1:T(1,128)S(1)} copy-done((f32[1,3,1536]{2,0,1:T(1,128)S(1)}, f32[1,3,1536]{2,0,1:T(1,128)}, u32[]{:S(2)}) %copy-start.2) | copy-done | bytes 18456
  13.2 0.0 copy-start.4
  13.2 0.0 copy-start.5
  13.2 8.3 %first_part.1 = (bf16[256,1536]{1,0:T(8,128)(2,1)S(1)}, f32[256,1536]{1,0:T(8,128)S(1)}, f32[256,1536]{1,0:T(8,128)S(1)}, f32[256,1536]{1,0:T(8,128)S(1)}, bf16[1536,4608]{1,0:T(8,128)(2,1)S(1)}) custom-call(bf16[256,1536]{1,0:T(8,128)(2,1)S(1)} %bitcast.11, f32[3,1,1536]{2,1,0:T(1,128)S(1)} %bitcast.13, bf16[1536,4608]{1,0:T(8,128)(2,1)} %bitcast.26), custom_call_target="tpu_custom_call" | custom-call | tf_op jit(solution)/shard_map/first_part/pallas_call | solution.py:180
  21.5 0.0 collective-permute-done.rest_0_
  21.5 0.0 slice-start
  21.5 0.0 copy-done.4
  21.5 0.0 copy-done.5
  21.5 0.0 slice-start.1
  21.6 0.0 copy-start.1
  21.6 0.6 arrived_part.2.rest_0_
  22.2 2.5 %collective-permute-done.1.rest_1_ = bf16[128,1536]{1,0:T(8,128)(2,1)S(1)} collective-permute-done((bf16[128,1536]{1,0:T(8,128)(2,1)}, bf16[128,1536]{1,0:T(8,128)(2,1)S(1)}, u32[]{:S(2)}, u32[]{:S(2)}) %collective-permute-start.1) | collective-permute-done | bytes 393248 | tf_op jit(solution)/shard_map/ppermute | solution.py:399
  24.7 0.0 collective-permute-done.2.rest_2_
  24.7 0.0 collective-permute-done.3.rest_3_
  24.7 0.0 slice-done
  24.7 0.0 slice-done.1
  24.7 0.0 copy-done.1
  24.7 0.0 copy-start.3
  24.7 9.2 %last_part.2 = (bf16[128,1536]{1,0:T(8,128)(2,1)S(1)}, bf16[128,1536]{1,0:T(8,128)(2,1)S(1)}, bf16[128,1536]{1,0:T(8,128)(2,1)S(1)}) custom-call(s32[4,16]{1,0:T(4,128)S(1)} %bitcast.22, s32[16]{0:T(128)S(1)} %copy-done.5, bf16[128,3072]{1,0:T(8,128)(2,1)S(1)} %arrived_part.2.rest_0_, bf16[128,1536]{1,0:T(8,128)(2,1)S(1)} %collective-permute-done.1.rest_1_, ...), custom_call_target="tpu_custom_call" | custom-call | tf_op jit(solution)/shard_map/last_part/pallas_call | solution.py:371
  33.9 0.1 collective-permute-start.4
  34.0 1.6 %collective-permute-start.5 = (bf16[128,1536]{1,0:T(8,128)(2,1)S(1)}, bf16[128,1536]{1,0:T(8,128)(2,1)S(1)}, u32[]{:S(2)}, u32[]{:S(2)}) collective-permute-start(bf16[128,1536]{1,0:T(8,128)(2,1)S(1)} %get-tuple-element.37), channel_id=1, source_target_pairs={{0,8},{8,16},{16,24},{24,0},{1,9},{9,17},{17,25},{25,1},{2,10},{10... | collective-permute-start | bytes 1179656 | tf_op jit(solution)/shard_map/ppermute | solution.py:412
  35.6 1.9 %collective-permute-start.8 = (bf16[128,1536]{1,0:T(8,128)(2,1)S(1)}, bf16[128,1536]{1,0:T(8,128)(2,1)S(1)}, u32[]{:S(2)}, u32[]{:S(2)}) collective-permute-start(bf16[128,1536]{1,0:T(8,128)(2,1)S(1)} %get-tuple-element.41), channel_id=1, source_target_pairs={{0,0},{1,2},{2,1},{3,4},{4,3},{5,6},{6,5},{7,7},{8,8},{9,10},{10,9... | collective-permute-start | bytes 1179656 | tf_op jit(solution)/shard_map/ppermute | solution.py:399
  37.5 3.7 %collective-permute-done.4.x_ref.refs_0_.a_ref = bf16[128,1536]{1,0:T(8,128)(2,1)S(1)} collective-permute-done((bf16[128,1536]{1,0:T(8,128)(2,1)S(1)}, bf16[128,1536]{1,0:T(8,128)(2,1)S(1)}, u32[]{:S(2)}, u32[]{:S(2)}) %collective-permute-start.4) | collective-permute-done | bytes 393248 | tf_op jit(solution)/shard_map/ppermute | solution.py:412
  41.2 0.0 copy-done.3
  41.2 2.3 %half_part.1.qkv_ref = bf16[128,4608]{1,0:T(8,128)(2,1)S(1)} custom-call(bf16[128,1536]{1,0:T(8,128)(2,1)S(1)} %collective-permute-done.4.x_ref.refs_0_.a_ref, f32[3,1,1536]{2,1,0:T(1,128)S(1)} %bitcast.16, bf16[1536,4608]{1,0:T(8,128)(2,1)S(1)} %get-tuple-element.28.rest_2_.rest_10_.w_ref.rest_4_.rest_8_), custom_call_target="tpu_custom_call" | custom-call | tf_op jit(solution)/shard_map/half_part/pallas_call | solution.py:199
  43.5 1.9 %collective-permute-done.5.refs_1_.b_ref = bf16[128,1536]{1,0:T(8,128)(2,1)S(1)} collective-permute-done((bf16[128,1536]{1,0:T(8,128)(2,1)S(1)}, bf16[128,1536]{1,0:T(8,128)(2,1)S(1)}, u32[]{:S(2)}, u32[]{:S(2)}) %collective-permute-start.5) | collective-permute-done | bytes 393248 | tf_op jit(solution)/shard_map/ppermute | solution.py:412
  45.4 0.7 %pick_blocks.3 = (bf16[128,1536]{1,0:T(8,128)(2,1)S(1)}, bf16[128,1536]{1,0:T(8,128)(2,1)S(1)}, bf16[128,1536]{1,0:T(8,128)(2,1)S(1)}) custom-call(s32[4,16]{1,0:T(4,128)S(1)} %bitcast.23, bf16[128,1536]{1,0:T(8,128)(2,1)S(1)} %collective-permute-done.4.x_ref.refs_0_.a_ref, bf16[128,1536]{1,0:T(8,128)(2,1)S(1)} %collective-permute-done.5.refs_1_.b_ref), custom_call_target="tpu_custom_call" | custom-call | tf_op jit(solution)/shard_map/pick_blocks/pallas_call | solution.py:74
  46.1 0.1 collective-permute-start.6
  46.2 0.1 collective-permute-start.7
  46.3 3.2 %collective-permute-done.8 = bf16[128,1536]{1,0:T(8,128)(2,1)S(1)} collective-permute-done((bf16[128,1536]{1,0:T(8,128)(2,1)S(1)}, bf16[128,1536]{1,0:T(8,128)(2,1)S(1)}, u32[]{:S(2)}, u32[]{:S(2)}) %collective-permute-start.8) | collective-permute-done | bytes 393248 | tf_op jit(solution)/shard_map/ppermute | solution.py:399
  49.5 0.0 collective-permute-start.9
  49.6 2.0 %collective-permute-start.10 = (bf16[128,1536]{1,0:T(8,128)(2,1)S(1)}, bf16[128,1536]{1,0:T(8,128)(2,1)S(1)}, u32[]{:S(2)}, u32[]{:S(2)}) collective-permute-start(bf16[128,1536]{1,0:T(8,128)(2,1)S(1)} %get-tuple-element.42), channel_id=1, source_target_pairs={{0,0},{1,1},{2,4},{3,5},{4,2},{5,3},{6,6},{7,7},{8,8},{9,9},{10,12... | collective-permute-start | bytes 1179656 | tf_op jit(solution)/shard_map/ppermute | solution.py:399
  51.5 3.5 %second_part.1 = (bf16[256,1536]{1,0:T(8,128)(2,1)S(1)}, bf16[256,1536]{1,0:T(8,128)(2,1)S(1)}, f32[256,1536]{1,0:T(8,128)S(1)}, f32[256,1536]{1,0:T(8,128)S(1)}, f32[256,1536]{1,0:T(8,128)S(1)}) custom-call(bf16[128,1536]{1,0:T(8,128)(2,1)S(1)} %collective-permute-done.4.x_ref.refs_0_.a_ref, bf16[128,1536]{1,0:T(8,128)(2,1)S(1)} %collective-permute-done.5.refs_1_.b_ref, ...), custom_call_target="tpu_custom_call" | custom-call | tf_op jit(solution)/shard_map/second_part/pallas_call | solution.py:224
  55.1 2.8 %collective-permute-done.6.rest_0_ = bf16[128,1536]{1,0:T(8,128)(2,1)S(1)} collective-permute-done((bf16[128,1536]{1,0:T(8,128)(2,1)S(1)}, bf16[128,1536]{1,0:T(8,128)(2,1)S(1)}, u32[]{:S(2)}, u32[]{:S(2)}) %collective-permute-start.6) | collective-permute-done | bytes 393248 | tf_op jit(solution)/shard_map/ppermute | solution.py:399
  57.9 0.0 collective-permute-done.7.rest_1_
  57.9 0.0 collective-permute-done.9.rest_2_
  57.9 4.2 %arrived_part.3.rest_0_ = bf16[384,3072]{1,0:T(8,128)(2,1)S(1)} custom-call(s32[4,16]{1,0:T(4,128)S(1)} %bitcast.24, s32[16]{0:T(128)S(1)} %copy-done.5, bf16[128,1536]{1,0:T(8,128)(2,1)S(1)} %collective-permute-done.6.rest_0_, bf16[128,1536]{1,0:T(8,128)(2,1)S(1)} %collective-permute-done.7.rest_1_, bf16[128,1536]{1,0:T(8,128)(2,1)S(1)} %collective-permute-done.9.rest_2_, ...), custom_call_target="tpu_custom_call" | custom-call | tf_op jit(solution)/shard_map/arrived_part/pallas_call | solution.py:267
  62.1 1.0 %collective-permute-done.10.rest_1_ = bf16[128,1536]{1,0:T(8,128)(2,1)S(1)} collective-permute-done((bf16[128,1536]{1,0:T(8,128)(2,1)S(1)}, bf16[128,1536]{1,0:T(8,128)(2,1)S(1)}, u32[]{:S(2)}, u32[]{:S(2)}) %collective-permute-start.10) | collective-permute-done | bytes 393248 | tf_op jit(solution)/shard_map/ppermute | solution.py:399
  63.1 6.3 %last_part.3 = bf16[256,1536]{1,0:T(8,128)(2,1)} custom-call(s32[4,16]{1,0:T(4,128)S(1)} %bitcast.25, s32[16]{0:T(128)S(1)} %copy-done.5, bf16[384,3072]{1,0:T(8,128)(2,1)S(1)} %arrived_part.3.rest_0_, bf16[128,1536]{1,0:T(8,128)(2,1)S(1)} %collective-permute-done.10.rest_1_, bf16[256,1536]{1,0:T(8,128)(2,1)S(1)} %get-tuple-element.44.rest_2_, ...), custom_call_target="tpu_custom_call" | custom-call | tf_op jit(solution)/shard_map/last_part/pallas_call | solution.py:371
  (1 shorter events, 0.0 us)
Async XLA Ops:
  2.4 19.1 %collective-permute-start = (bf16[128,1536]{1,0:T(8,128)(2,1)}, bf16[128,1536]{1,0:T(8,128)(2,1)S(1)}, u32[]{:S(2)}, u32[]{:S(2)}) collective-permute-start(bf16[128,1536]{1,0:T(8,128)(2,1)} %get-tuple-element.27), channel_id=1, source_target_pairs={{0,0},{1,2},{2,1},{3,4},{4,3},{5,6},{6,5},{7,7},{8,8},{9,10},{10,9... | collective-permute-start | bytes 1179656 | tf_op jit(solution)/shard_map/ppermute | solution.py:399
  5.8 18.8 %collective-permute-start.1 = (bf16[128,1536]{1,0:T(8,128)(2,1)}, bf16[128,1536]{1,0:T(8,128)(2,1)S(1)}, u32[]{:S(2)}, u32[]{:S(2)}) collective-permute-start(bf16[128,1536]{1,0:T(8,128)(2,1)} %get-tuple-element.29), channel_id=1, source_target_pairs={{0,1},{1,0},{2,3},{3,2},{4,5},{5,4},{6,7},{7,6},{8,9},{9,8},{10,11... | collective-permute-start | bytes 1179656 | tf_op jit(solution)/shard_map/ppermute | solution.py:399
  6.3 18.4 %collective-permute-start.2 = (bf16[128,1536]{1,0:T(8,128)(2,1)}, bf16[128,1536]{1,0:T(8,128)(2,1)S(1)}, u32[]{:S(2)}, u32[]{:S(2)}) collective-permute-start(bf16[128,1536]{1,0:T(8,128)(2,1)} %get-tuple-element.30), channel_id=1, source_target_pairs={{0,2},{1,3},{2,0},{3,1},{4,6},{5,7},{6,4},{7,5},{8,10},{9,11},{10,... | collective-permute-start | bytes 1179656 | tf_op jit(solution)/shard_map/ppermute | solution.py:399
  6.4 18.3 %collective-permute-start.3 = (bf16[128,1536]{1,0:T(8,128)(2,1)}, bf16[128,1536]{1,0:T(8,128)(2,1)S(1)}, u32[]{:S(2)}, u32[]{:S(2)}) collective-permute-start(bf16[128,1536]{1,0:T(8,128)(2,1)} %get-tuple-element.31), channel_id=1, source_target_pairs={{0,0},{1,1},{2,4},{3,5},{4,2},{5,3},{6,6},{7,7},{8,8},{9,9},{10,12... | collective-permute-start | bytes 1179656 | tf_op jit(solution)/shard_map/ppermute | solution.py:399
  11.4 1.1 %copy-start = (bf16[1,256,1536]{2,1,0:T(8,128)(2,1)S(1)}, bf16[1,256,1536]{2,1,0:T(8,128)(2,1)}, u32[]{:S(2)}) copy-start(bf16[1,256,1536]{2,1,0:T(8,128)(2,1)} %param.6) | copy-start | bytes 2359300
  12.5 0.7 %copy-start.2 = (f32[1,3,1536]{2,0,1:T(1,128)S(1)}, f32[1,3,1536]{2,0,1:T(1,128)}, u32[]{:S(2)}) copy-start(f32[1,3,1536]{2,0,1:T(1,128)} %param.9) | copy-start | bytes 55300
  13.2 8.3 %copy-start.4 = (s32[16,4]{0,1:T(4,128)S(1)}, s32[16,4]{0,1:T(4,128)}, u32[]{:S(2)}) copy-start(s32[16,4]{0,1:T(4,128)} %param.10) | copy-start | bytes 772
  13.2 8.3 %copy-start.5 = (s32[16]{0:T(128)S(1)}, s32[16]{0:T(128)}, u32[]{:S(2)}) copy-start(s32[16]{0:T(128)} %count_ref.7) | copy-start | bytes 196
  21.5 3.2 %slice-start = ((s8[4718592]{0:T(1024)(128)(4,1)}), s8[4194304]{0:T(1024)(128)(4,1)S(1)}, s32[]{:S(2)}) async-start(s8[4718592]{0:T(1024)(128)(4,1)} %bitcast.6), calls=%async_computation | async-start | bytes 8388608
  21.5 3.2 %slice-start.1 = ((s8[4718592]{0:T(1024)(128)(4,1)}), s8[524288]{0:T(1024)(128)(4,1)S(1)}, s32[]{:S(2)}) async-start(s8[4718592]{0:T(1024)(128)(4,1)} %bitcast.6), calls=%async_computation.1 | async-start | bytes 1048576
  21.6 3.2 %copy-start.1 = (bf16[1,256,1536]{2,1,0:T(8,128)(2,1)S(1)}, bf16[1,256,1536]{2,1,0:T(8,128)(2,1)}, u32[]{:S(2)}) copy-start(bf16[1,256,1536]{2,1,0:T(8,128)(2,1)} %param.6) | copy-start | bytes 2359300
  24.7 16.4 %copy-start.3 = (f32[1,3,1536]{2,0,1:T(1,128)S(1)}, f32[1,3,1536]{2,0,1:T(1,128)}, u32[]{:S(2)}) copy-start(f32[1,3,1536]{2,0,1:T(1,128)} %param.9) | copy-start | bytes 55300
  33.9 7.3 %collective-permute-start.4 = (bf16[128,1536]{1,0:T(8,128)(2,1)S(1)}, bf16[128,1536]{1,0:T(8,128)(2,1)S(1)}, u32[]{:S(2)}, u32[]{:S(2)}) collective-permute-start(bf16[128,1536]{1,0:T(8,128)(2,1)S(1)} %get-tuple-element.36), channel_id=1, source_target_pairs={{0,8},{8,16},{16,24},{24,0},{1,9},{9,17},{17,25},{25,1},{2,10},{10... | collective-permute-start | bytes 1179656 | tf_op jit(solution)/shard_map/ppermute | solution.py:412
  34.0 11.4 %collective-permute-start.5 = (bf16[128,1536]{1,0:T(8,128)(2,1)S(1)}, bf16[128,1536]{1,0:T(8,128)(2,1)S(1)}, u32[]{:S(2)}, u32[]{:S(2)}) collective-permute-start(bf16[128,1536]{1,0:T(8,128)(2,1)S(1)} %get-tuple-element.37), channel_id=1, source_target_pairs={{0,8},{8,16},{16,24},{24,0},{1,9},{9,17},{17,25},{25,1},{2,10},{10... | collective-permute-start | bytes 1179656 | tf_op jit(solution)/shard_map/ppermute | solution.py:412
  35.6 14.0 %collective-permute-start.8 = (bf16[128,1536]{1,0:T(8,128)(2,1)S(1)}, bf16[128,1536]{1,0:T(8,128)(2,1)S(1)}, u32[]{:S(2)}, u32[]{:S(2)}) collective-permute-start(bf16[128,1536]{1,0:T(8,128)(2,1)S(1)} %get-tuple-element.41), channel_id=1, source_target_pairs={{0,0},{1,2},{2,1},{3,4},{4,3},{5,6},{6,5},{7,7},{8,8},{9,10},{10,9... | collective-permute-start | bytes 1179656 | tf_op jit(solution)/shard_map/ppermute | solution.py:399
  46.1 11.7 %collective-permute-start.6 = (bf16[128,1536]{1,0:T(8,128)(2,1)S(1)}, bf16[128,1536]{1,0:T(8,128)(2,1)S(1)}, u32[]{:S(2)}, u32[]{:S(2)}) collective-permute-start(bf16[128,1536]{1,0:T(8,128)(2,1)S(1)} %get-tuple-element.39), channel_id=1, source_target_pairs={{0,1},{1,0},{2,3},{3,2},{4,5},{5,4},{6,7},{7,6},{8,9},{9,8},{10,11... | collective-permute-start | bytes 1179656 | tf_op jit(solution)/shard_map/ppermute | solution.py:399
  46.2 11.6 %collective-permute-start.7 = (bf16[128,1536]{1,0:T(8,128)(2,1)S(1)}, bf16[128,1536]{1,0:T(8,128)(2,1)S(1)}, u32[]{:S(2)}, u32[]{:S(2)}) collective-permute-start(bf16[128,1536]{1,0:T(8,128)(2,1)S(1)} %get-tuple-element.40), channel_id=1, source_target_pairs={{0,2},{1,3},{2,0},{3,1},{4,6},{5,7},{6,4},{7,5},{8,10},{9,11},{10,... | collective-permute-start | bytes 1179656 | tf_op jit(solution)/shard_map/ppermute | solution.py:399
  49.5 8.3 %collective-permute-start.9 = (bf16[128,1536]{1,0:T(8,128)(2,1)S(1)}, bf16[128,1536]{1,0:T(8,128)(2,1)S(1)}, u32[]{:S(2)}, u32[]{:S(2)}) collective-permute-start(bf16[128,1536]{1,0:T(8,128)(2,1)S(1)} %collective-permute-done.8), channel_id=1, source_target_pairs={{0,8},{8,16},{16,24},{24,0},{1,9},{9,17},{17,25},{25,1},{2,10},{10... | collective-permute-start | bytes 1179656 | tf_op jit(solution)/shard_map/ppermute | solution.py:414
  49.6 13.6 %collective-permute-start.10 = (bf16[128,1536]{1,0:T(8,128)(2,1)S(1)}, bf16[128,1536]{1,0:T(8,128)(2,1)S(1)}, u32[]{:S(2)}, u32[]{:S(2)}) collective-permute-start(bf16[128,1536]{1,0:T(8,128)(2,1)S(1)} %get-tuple-element.42), channel_id=1, source_target_pairs={{0,0},{1,1},{2,4},{3,5},{4,2},{5,3},{6,6},{7,7},{8,8},{9,9},{10,12... | collective-permute-start | bytes 1179656 | tf_op jit(solution)/shard_map/ppermute | solution.py:399
